TPU v7x, 32 devices: a whole 2x2x4 slice. The times are simulated.
32 devices in a mesh: parts: 2 (over x), gx: 4 (over y, core), gy: 4 (over z).
Axes of the slice: x: 2, y: 2, z: 4, core: 2. Of those that a mesh axis runs over, the one named last changes fastest.
Arguments:
- forcing_right_side: float32 [32, 32, 1024], P(('parts', 'gx'), 'gy'), parts along dimension 0, may hold values from -18 to 18
- earlier_warmth: float32 [32, 32, 1024], P(('parts', 'gx'), 'gy'), parts along dimension 0, may hold values from 0 to 2
- matter_condition: int32 [32, 32, 1024], P(('parts', 'gx'), 'gy'), parts along dimension 0, may hold values from 0 to 2
- compressed_slot_number: int32 [32, 32, 1024], P(('parts', 'gx'), 'gy'), parts along dimension 0, may hold values from 0 to 127
- normal_draw_factor: float32 [32, 32, 1024], P(('parts', 'gx'), 'gy'), parts along dimension 0, may hold values from -6 to 6
Outputs:
- solution: float32 [32, 32, 1024], P(('parts', 'gx'), 'gy'), parts along dimension 0
- residual: float32 [32, 32, 1024], P(('parts', 'gx'), 'gy'), parts along dimension 0
There are 2 independent parts, one for each index of `parts`. A program takes and returns all parts, laid end to end along the dimension named above; each array names one. Nothing has to cross between parts.
Inputs may be any that keep to these rules, and one draw needn't show every extreme that they name: `matter_condition`: phase labels the cell as powder, solid or liquid. `compressed_slot_number`: each cell's row of the sketch.
All inputs are finite; a program needn't handle non-finite values.
Results may differ from a plain program's by a relative error of at most 0.0003.
Values sent between devices are 32-bit elements; how exact they have to be, the bound alone decides.
No kernel may reach another device: no remote copies, remote signals or barrier semaphores. Data moves between devices by JAX's collectives and lax.ppermute only.
A program may use at most 64 MiB of HBM per device.

v0:
```python
import jax
import jax.numpy as jnp
from jax import lax
from jax.experimental import pallas as pl
from jax.experimental.pallas import tpu as pltpu
from jax.sharding import PartitionSpec as P

SKETCH = 128
LOW = 32
HIGH = SKETCH // LOW
FIELDS = 3
LANES = 128
epsilon = 1e-06


def traits(warmth, phase):
    powder, solid = phase == 0, phase == 1
    offset = jnp.where(powder, 0.2, jnp.where(solid, 1.0, 0.6))
    return offset * (0.5 + warmth), jnp.where(powder, 1.0, jnp.where(solid, 2.0, 1.5))


def link(first, second):
    total = first + second
    return 2.0 * first * second / jnp.where(total > 0.0, total, 1.0)


def ahead(plane, axis):
    return pltpu.roll(plane, plane.shape[axis] - 1, axis)


def inner_links(cond):
    links = []
    for axis in (0, 1):
        index = lax.broadcasted_iota(jnp.int32, cond.shape, axis)
        links.append(
            jnp.where(index < cond.shape[axis] - 1, link(cond, ahead(cond, axis)), 0.0)
        )
    return links


def inner_flow(field, links):
    total = None
    for axis in (0, 1):
        flow = links[axis] * (field - ahead(field, axis))
        part = flow - pltpu.roll(flow, 1, axis)
        total = part if total is None else total + part
    return total


def apply_inside(images, c_wide, caps):
    results = []
    flow_low = link(c_wide[0], c_wide[1]) * (images[0] - images[1])
    for i in range(1, len(images) - 1):
        image = images[i]
        flow = link(c_wide[i], c_wide[i + 1]) * (image - images[i + 1])
        results.append(
            caps[i - 1] * image + inner_flow(image, inner_links(c_wide[i])) + (flow - flow_low)
        )
        flow_low = flow
    return results


def sketch_rows(planes, cells_ref):
    depth = cells_ref.shape[0] * LANES
    low_index = lax.broadcasted_iota(jnp.int32, (LOW, depth), 0)
    low_index = low_index.astype(jnp.float32).astype(jnp.bfloat16)
    high_index = lax.broadcasted_iota(jnp.int32, (HIGH * 8, depth), 0) // 8
    high_index = high_index.astype(jnp.float32).astype(jnp.bfloat16)
    total = jnp.zeros((HIGH * 8, LOW), jnp.float32)
    start = 0
    for fields, draw, slot, chosen in planes:
        rows = draw.shape[0]
        coarse, fine = [], []
        for field in fields:
            weighted = draw * field
            head = weighted.astype(jnp.bfloat16).astype(jnp.float32)
            coarse.append(head)
            fine.append(weighted - head)
        for f, part in enumerate(coarse + coarse[:1] + fine + fine[:1]):
            for t in range(depth // LANES):
                cells_ref[t, pl.ds(start + f, rows, stride=8), :] = part[
                    :, t * LANES : (t + 1) * LANES
                ]
        high = jnp.floor(slot * (1.0 / LOW))
        low = slot - LOW * high
        left, right = [], []
        for j in chosen:
            at = pl.ds(start + j * 8, 8)
            cells = [cells_ref[t, at, :] for t in range(depth // LANES)]
            cells = jnp.concatenate(cells, axis=1)
            cells = jnp.concatenate([cells] * HIGH, axis=0).astype(jnp.bfloat16)
            row_high = jnp.broadcast_to(high[j : j + 1], cells.shape).astype(jnp.bfloat16)
            row_low = jnp.broadcast_to(low[j : j + 1], (LOW, depth)).astype(jnp.bfloat16)
            left.append(jnp.where(row_high == high_index, cells, jnp.zeros_like(cells)))
            right.append(
                jnp.where(row_low == low_index, jnp.ones_like(row_low), jnp.zeros_like(row_low))
            )
        total = total + lax.dot_general(
            jnp.concatenate(left, axis=1),
            jnp.concatenate(right, axis=1),
            (((1,), (1,)), ((), ())),
            preferred_element_type=jnp.float32,
        )
        start += rows * 8
    parts = jnp.concatenate([total[h * 8 : h * 8 + 8] for h in range(HIGH)], axis=1)
    return parts + pltpu.roll(parts, 4, 0)


def first_kernel(
    b_hbm, warmth_hbm, phase_hbm, draw_hbm, slot_hbm, b_ref, cond_ref, cap_ref, inner_ref,
    draw_ref, slot_ref, x_first_ref, x_second_ref, y_first_ref, y_second_ref, warmth_ref,
    phase_ref, number_ref, arrived,
):
    copies = [
        pltpu.make_async_copy(source, target, arrived.at[k])
        for k, (source, target) in enumerate(
            (
                (b_hbm, b_ref),
                (warmth_hbm, warmth_ref),
                (phase_hbm, phase_ref),
                (draw_hbm, draw_ref),
                (slot_hbm, number_ref),
            )
        )
    ]
    for copy in copies:
        copy.start()
    for copy in copies[:3]:
        copy.wait()
    planes, rows = b_ref.shape[:2]
    images, conds = [], []
    for i in range(planes):
        cond, cap = traits(warmth_ref[i], phase_ref[i])
        cap_ref[i] = cap
        cond_ref[i] = cond
        field = b_ref[i]
        image = cap * field + inner_flow(field, inner_links(cond))
        if i:
            flow = link(conds[-1], cond) * (b_ref[i - 1] - field)
            images[-1] = images[-1] + flow
            image = image - flow
        conds.append(cond)
        images.append(image)
    for i in range(planes):
        inner_ref[i] = images[i]
    for k, field in enumerate((images, [b_ref[i] for i in range(planes)], conds)):
        at = slice(k * rows, (k + 1) * rows)
        x_first_ref[at], x_second_ref[at] = by_turn(field[0], field[-1], "gx")
        for i, plane in enumerate(field):
            at = slice(k * planes + i, k * planes + i + 1)
            y_first_ref[at], y_second_ref[at] = by_turn(plane[:1], plane[rows - 1 :], "gy")
    for copy in copies[3:]:
        copy.wait()
    for i in range(planes):
        slot_ref[i] = number_ref[i].astype(jnp.float32)
    for k, ref in enumerate((draw_ref, slot_ref)):
        ends = [ref[0], ref[planes - 1]]
        for e, j in enumerate((0, rows - 1)):
            at = slice(3 * rows + 2 * k + e, 3 * rows + 2 * k + e + 1)
            lines = [plane[j : j + 1] for plane in ends]
            x_first_ref[at], x_second_ref[at] = by_turn(*lines, "gx")
        for e, plane in enumerate(ends):
            at = slice(3 * planes + 2 * k + e, 3 * planes + 2 * k + e + 1)
            lines = [plane[:1], plane[rows - 1 :]]
            y_first_ref[at], y_second_ref[at] = by_turn(*lines, "gy")


def by_turn(one, other, axis):
    odd = lax.axis_index(axis) % 2 == 1
    return jnp.where(odd, one, other), jnp.where(odd, other, one)


def has_beside(axis):
    at = lax.axis_index(axis)
    return at > 0, at < lax.axis_size(axis) - 1


def reached(rows):
    others = [j for j in range(rows) if 2 <= j < rows - 2]
    return [j for j in range(rows) if j not in others], others


def widened(ref, beside_ref, which):
    inner = [ref[i] for i in range(ref.shape[0])]
    return [beside_ref[which]] + inner + [beside_ref[which + 1]]


def inside_kernel(
    b_ref, cond_ref, cap_ref, inner_ref, draw_ref, slot_ref, got_second_ref, got_first_ref,
    wide_ref, beside_ref, sketch_ref, cells_ref,
):
    planes, rows = b_ref.shape[:2]
    (image_low, image_high), (b_low, b_high), (c_low, c_high) = (
        by_turn(*(ref[k * rows : (k + 1) * rows] for ref in (got_first_ref, got_second_ref)), "gx")
        for k in range(3)
    )
    below, above = has_beside("gx")
    c_low, c_high = jnp.where(below, c_low, 0.0), jnp.where(above, c_high, 0.0)
    for k, plane in enumerate((b_low, b_high, c_low, c_high)):
        beside_ref[k] = plane
    c_wide = [c_low] + [cond_ref[i] for i in range(planes)] + [c_high]
    low_flow = link(c_low, c_wide[1]) * (b_low - b_ref[0])
    high_flow = link(c_wide[-2], c_high) * (b_ref[planes - 1] - b_high)
    images = [image_low + low_flow] + [inner_ref[i] for i in range(planes)]
    images.append(image_high - high_flow)
    images[1] = images[1] - low_flow
    images[-2] = images[-2] + high_flow
    for i, image in enumerate(images):
        wide_ref[i] = image
    twice = apply_inside(images, c_wide, [cap_ref[i] for i in range(planes)])
    chosen = reached(rows)[1]
    sketch_ref[...] = sketch_rows(
        [
            ((b_ref[i], images[i + 1], twice[i]), draw_ref[i], slot_ref[i], chosen)
            for i in range(planes)
        ],
        cells_ref,
    )


def third_kernel(
    b_ref, cond_ref, cap_ref, draw_ref, slot_ref, wide_ref, beside_ref, x_second_ref,
    x_first_ref, y_second_ref, y_first_ref, inside_ref, image_ref, twice_ref, sketch_ref,
    corner_first_ref, corner_second_ref, ends_ref, cells_ref, extra_ref,
):
    planes, rows, depth = b_ref.shape
    index = lax.broadcasted_iota(jnp.int32, (rows, depth), 0)
    b_wide = widened(b_ref, beside_ref, 0)
    c_wide = widened(cond_ref, beside_ref, 2)
    images = [wide_ref[i] for i in range(planes + 2)]
    x_ends = []
    for inner, outer in ((1, 0), (planes, planes + 1)):
        conductance = link(c_wide[inner], c_wide[outer])
        x_ends.append((inner, outer, conductance, conductance * (b_wide[inner] - b_wide[outer])))
    x_tails = by_turn(x_first_ref[3 * rows :], x_second_ref[3 * rows :], "gx")
    y_lines = by_turn(y_first_ref[...], y_second_ref[...], "gy")
    beside = []
    for side, (j, here, line) in enumerate(zip((0, rows - 1), has_beside("gy"), y_lines)):
        row = slice(j, j + 1)
        parts = [[line[k * planes + i :][:1] for i in range(planes)] for k in range(3)]
        beyond, b_line, c_line = parts
        c_line = [jnp.where(here, c, 0.0) for c in c_line]
        flows = []
        for i in range(planes):
            conductance = link(c_wide[i + 1], jnp.broadcast_to(c_line[i], (rows, depth)))
            conductance = jnp.where(index == j, conductance, 0.0)
            flow = conductance * (b_wide[i + 1] - b_line[i])
            images[i + 1] = images[i + 1] + flow
            beside.append((i, conductance, beyond[i] - flow))
            flows.append((conductance, flow))
        for end, (inner, outer, x_link, x_flow) in enumerate(x_ends):
            y_link, y_flow = flows[inner - 1]
            at = 4 * side + 2 * end
            tail = x_tails[end]
            values = (-x_link * y_flow)[row], tail[side : side + 1], tail[2 + side : 3 + side]
            for k, value in enumerate(values):
                extra_ref[k, at : at + 1] = value
            tail = line[3 * planes :]
            values = (-y_link * x_flow)[row], tail[end : end + 1], tail[2 + end : 3 + end]
            for k, value in enumerate(values):
                extra_ref[k, at + 1 : at + 2] = value
            at = 6 * (2 * side + end)
            values = x_link, b_wide[outer], c_wide[outer], y_link
            for k, value in enumerate(values):
                ends_ref[at + k : at + k + 1] = value[row]
            ends_ref[at + 4 : at + 5] = b_line[inner - 1]
            ends_ref[at + 5 : at + 6] = c_line[inner - 1]
    twice = apply_inside(images, c_wide, [cap_ref[i] for i in range(planes)])
    for i, conductance, value in beside:
        twice[i] = twice[i] + conductance * (images[i + 1] - value)
    for i in range(planes):
        image_ref[i] = images[i + 1]
        twice_ref[i] = twice[i]
    chosen = reached(rows)[0]
    cells = [
        ((b_wide[i + 1], images[i + 1], twice[i]), draw_ref[i], slot_ref[i], chosen)
        for i in range(planes)
    ]
    extra, nothing = [extra_ref[k] for k in range(3)], jnp.zeros((8, depth), jnp.float32)
    cells.append(((nothing, nothing, extra[0]), extra[1], extra[2], range(8)))
    sketch = inside_ref[...] + sketch_rows(cells, cells_ref)
    sketch_ref[...] = sketch[: FIELDS + 1]
    for k, plane in enumerate((b_wide[0], b_wide[-1], c_wide[0], c_wide[-1])):
        at = slice(k, k + 1)
        corner_first_ref[at], corner_second_ref[at] = by_turn(
            plane[:1], plane[rows - 1 :], "gy"
        )


def last_kernel(
    sketch_ref, b_ref, image_ref, twice_ref, ends_ref, corner_first_ref, corner_second_ref,
    solution_ref, residual_ref,
):
    sketches = jnp.sum(sketch_ref[...], axis=0)

    def inner(first, second):
        return jnp.sum(first * second, axis=1, keepdims=True)

    s0, s1, s2 = (sketches[i : i + 1] for i in range(FIELDS))
    beta = jnp.sqrt(inner(s0, s0) + epsilon)
    q0 = s0 / beta
    p0 = s1 / beta
    h00 = inner(q0, p0)
    t0 = p0 - h00 * q0
    n0 = jnp.sqrt(inner(t0, t0) + epsilon)
    q1 = t0 / n0
    p1 = (s2 / beta - h00 * p0) / n0
    h01 = inner(q0, p1)
    h11 = inner(q1, p1)
    t1 = p1 - h01 * q0 - h11 * q1
    n1 = jnp.sqrt(inner(t1, t1) + epsilon)
    l00 = jnp.sqrt(h00 * h00 + n0 * n0)
    l10 = (h00 * h01 + n0 * h11) / l00
    l11 = jnp.sqrt(h01 * h01 + h11 * h11 + n1 * n1 - l10 * l10)
    z0 = beta * h00 / l00
    z1 = (beta * h01 - l10 * z0) / l11
    y1 = z1 / l11
    y0 = (z0 - l10 * y1) / l00
    c1 = y1 / (beta * n0)
    c0 = y0 / beta - h00 * c1
    planes, rows, depth = b_ref.shape
    for i in range(planes):
        b, image = b_ref[i], image_ref[i]
        solution_ref[i] = c0 * b + c1 * image
        residual_ref[i] = b - c0 * image - c1 * twice_ref[i]
    corners = by_turn(corner_first_ref[...], corner_second_ref[...], "gy")
    for side, (j, here, corner) in enumerate(zip((0, rows - 1), has_beside("gy"), corners)):
        for end, i in enumerate((0, planes - 1)):
            b, cond = corner[end : end + 1], corner[2 + end : 3 + end]
            cond = jnp.where(here, cond, 0.0)
            at = 6 * (2 * side + end)
            x_link, x_b, x_cond, y_link, y_b, y_cond = (
                ends_ref[at + k : at + k + 1] for k in range(6)
            )
            lacked = x_link * link(x_cond, cond) * (x_b - b)
            lacked = lacked + y_link * link(y_cond, cond) * (y_b - b)
            residual_ref[i, j : j + 1] = residual_ref[i, j : j + 1] + c1 * lacked


def call(kernel, shapes, *operands, scratch=(), inputs=pltpu.VMEM, flops=0):
    return pl.pallas_call(
        kernel,
        out_shape=[jax.ShapeDtypeStruct(shape, jnp.float32) for shape in shapes],
        in_specs=[pl.BlockSpec(memory_space=inputs)] * len(operands),
        out_specs=[pl.BlockSpec(memory_space=pltpu.VMEM)] * len(shapes),
        scratch_shapes=scratch,
        compiler_params=pltpu.CompilerParams(vmem_limit_bytes=48 * 1024 * 1024),
        cost_estimate=pl.CostEstimate(flops=flops, bytes_accessed=0, transcendentals=0),
    )(*operands)


def swap(array, axis, turn):
    nx, ny = lax.axis_size("gx"), lax.axis_size("gy")
    pairs = []
    for x in range(nx):
        for y in range(ny):
            here, count = (x, nx) if axis == "gx" else (y, ny)
            there = here + 1 if here % 2 == turn else here - 1
            if 0 <= there < count:
                partner = (there, y) if axis == "gx" else (x, there)
            else:
                partner = (x, y ^ 1) if axis == "gx" else (x ^ 1, y)
            pairs.append((x * ny + y, partner[0] * ny + partner[1]))
    return lax.ppermute(array, ("gx", "gy"), pairs)


def everyones(sketch):
    count = lax.axis_size("gx") * lax.axis_size("gy")
    copies = jnp.broadcast_to(sketch[None], (count,) + sketch.shape)
    return lax.all_to_all(copies, ("gx", "gy"), 0, 0)


def body(b, warmth, phase, slots, draw):
    planes, rows, depth = b.shape
    block, wide, table = b.shape, (planes + 2, rows, depth), (8, SKETCH)
    face, line, corner = (3 * rows + 4, depth), (3 * planes + 4, depth), (4, depth)
    cells = pltpu.VMEM((depth // LANES, (planes * rows + 8) * 8, LANES), jnp.float32)
    work = b.size * SKETCH * 6
    b, cond, cap, inner, draw, slots, x_first, x_second, y_first, y_second = call(
        first_kernel,
        [block] * 6 + [face, face, line, line],
        *(
            pltpu.with_memory_space_constraint(x, pltpu.HBM)
            for x in (b, warmth, phase, draw, slots)
        ),
        scratch=[
            pltpu.VMEM(block, warmth.dtype),
            pltpu.VMEM(block, phase.dtype),
            pltpu.VMEM(block, slots.dtype),
            pltpu.SemaphoreType.DMA((5,)),
        ],
        inputs=pltpu.HBM,
    )
    x_second = swap(x_second, "gx", 1)
    got_y = swap(y_second, "gy", 1), swap(y_first, "gy", 0)
    got_x = x_second, swap(x_first, "gx", 0)
    image_wide, beside, inside = call(
        inside_kernel,
        [wide, (4, rows, depth), table],
        b, cond, cap, inner, draw, slots, *got_x,
        scratch=[cells],
        flops=work,
    )
    image, twice, sketch, first, second, ends = call(
        third_kernel,
        [block, block, (FIELDS + 1, SKETCH), corner, corner, (24, depth)],
        b, cond, cap, draw, slots, image_wide, beside, *got_x, *got_y, inside,
        scratch=[cells, pltpu.VMEM((3, 8, depth), jnp.float32)],
        flops=work,
    )
    got_corners = [swap(array, "gy", turn) for turn, array in enumerate((first, second))]
    sketches = everyones(sketch)
    return tuple(
        call(last_kernel, [block, block], sketches, b, image, twice, ends, *got_corners)
    )


def solution(mesh):
    spec = P(("parts", "gx"), "gy", None)
    return jax.shard_map(
        body, mesh=mesh, in_specs=(spec,) * 5, out_specs=(spec,) * 2, check_vma=False
    )
```

profile of v0, /device:TPU:0, one launch (start us, length us, event | category | flops | bytes accessed | tf_op | source)
XLA Modules:
  0.0 24.6 jit_solution(16538070556321533302)
XLA Ops:
  0.6 1.5 %shard_map.68 = (f32[4,8,1024]{2,1,0:T(8,128)S(1)}, f32[4,8,1024]{2,1,0:T(8,128)S(1)}, f32[4,8,1024]{2,1,0:T(8,128)S(1)}, f32[4,8,1024]{2,1,0:T(8,128)S(1)}, f32...) custom-call(f32[4,8,1024]{2,1,0:T(8,128)} %b_hbm.1, ...), custom_call_target="tpu_custom_call" | custom-call | tf_op jit(solution)/shard_map/pallas_call | solution.py:341
  2.1 3.1 %collective-permute-start = (f32[28,1024]{1,0:T(8,128)S(1)}, f32[28,1024]{1,0:T(8,128)S(1)}, u32[]{:S(2)}, u32[]{:S(2)}) collective-permute-start(f32[28,1024]{1,0:T(8,128)S(1)} %get-tuple-element.27), channel_id=1, source_target_pairs={{0,1},{1,0},{2,3},{3,2},{4,8},{5,9},{6,10},{7,11},{8,4},{9,5},{10,... | collective-permute-start | bytes 344072 | tf_op jit(solution)/shard_map/ppermute | solution.py:364
  5.2 0.1 collective-permute-start.1
  5.2 0.5 %collective-permute-start.2 = (f32[16,1024]{1,0:T(8,128)S(1)}, f32[16,1024]{1,0:T(8,128)S(1)}, u32[]{:S(2)}, u32[]{:S(2)}) collective-permute-start(f32[16,1024]{1,0:T(8,128)S(1)} %get-tuple-element.31), channel_id=1, source_target_pairs={{0,4},{1,2},{2,1},{3,7},{4,0},{5,6},{6,5},{7,3},{8,12},{9,10},{10,... | collective-permute-start | bytes 196616 | tf_op jit(solution)/shard_map/ppermute | solution.py:364
  5.7 2.7 %collective-permute-start.3 = (f32[16,1024]{1,0:T(8,128)S(1)}, f32[16,1024]{1,0:T(8,128)S(1)}, u32[]{:S(2)}, u32[]{:S(2)}) collective-permute-start(f32[16,1024]{1,0:T(8,128)S(1)} %get-tuple-element.32), channel_id=1, source_target_pairs={{0,1},{1,0},{2,3},{3,2},{4,5},{5,4},{6,7},{7,6},{8,9},{9,8},{10,11... | collective-permute-start | bytes 196616 | tf_op jit(solution)/shard_map/ppermute | solution.py:364
  8.4 0.0 collective-permute-done.got_second_ref.x_second_ref
  8.4 0.0 collective-permute-done.1.got_first_ref.x_first_ref
  8.4 0.8 %shard_map.69 = (f32[6,8,1024]{2,1,0:T(8,128)S(1)}, f32[4,8,1024]{2,1,0:T(8,128)S(1)}, f32[8,128]{1,0:T(8,128)S(1)}) custom-call(f32[4,8,1024]{2,1,0:T(8,128)S(1)} %get-tuple-element.21.b_ref, f32[4,8,1024]{2,1,0:T(8,128)S(1)} %get-tuple-element.22.cond_ref, f32[4,8,1024]{2,1,0:T(8,128)S(1)} %get-tuple-element.23.cap_ref, ...), custom_call_target="tpu_custom_call" | custom-call | flops 25165824 | tf_op jit(solution)/shard_map/pallas_call | solution.py:341
  9.2 0.0 collective-permute-done.2.y_second_ref
  9.2 1.6 %collective-permute-done.3.y_first_ref = f32[16,1024]{1,0:T(8,128)S(1)} collective-permute-done((f32[16,1024]{1,0:T(8,128)S(1)}, f32[16,1024]{1,0:T(8,128)S(1)}, u32[]{:S(2)}, u32[]{:S(2)}) %collective-permute-start.3) | collective-permute-done | bytes 65568 | tf_op jit(solution)/shard_map/ppermute | solution.py:364
  10.8 1.2 %shard_map.70 = (f32[4,8,1024]{2,1,0:T(8,128)S(1)}, f32[4,8,1024]{2,1,0:T(8,128)S(1)}, f32[4,128]{1,0:T(4,128)S(1)}, f32[4,1024]{1,0:T(4,128)S(1)}, f32[4,1024]{1,0:T(4,128)S(1)}, /*index=5*/f32[24,1024]{1,0:T(8,128)S(1)}) custom-call(f32[4,8,1024]{2,1,0:T(8,128)S(1)} %get-tuple-element.21.b_ref, f32[4,8,1024]{2,1,0:T(8,128)S(1)} %get-tuple-element.22.cond_ref, ...), custom_call_target="tpu_custom_call" | custom-call | flops 25165824 | tf_op jit(solution)/shard_map/pallas_call | solution.py:341
  12.1 0.6 %broadcast_in_dim.2 = f32[16,4,128]{2,1,0:T(4,128)} broadcast(f32[4,128]{1,0:T(4,128)S(1)} %get-tuple-element.34), dimensions={1,2} | broadcast | bytes 34816 | tf_op jit(solution)/shard_map/broadcast_in_dim | solution.py:369
  12.7 4.1 %all-to-all-start = ((f32[16,4,128]{2,1,0:T(4,128)}), f32[16,4,128]{2,1,0:T(4,128)S(1)}, u32[]{:S(2)}, u32[]{:S(2)}) async-start(f32[16,4,128]{2,1,0:T(4,128)} %broadcast_in_dim.2), calls=%async_computation | async-start | bytes 65536 | tf_op jit(solution)/shard_map/all_to_all | solution.py:370
  16.9 1.9 %collective-permute-start.4 = (f32[4,1024]{1,0:T(4,128)S(1)}, f32[4,1024]{1,0:T(4,128)S(1)}, u32[]{:S(2)}, u32[]{:S(2)}) collective-permute-start(f32[4,1024]{1,0:T(4,128)S(1)} %get-tuple-element.38), channel_id=1, source_target_pairs={{0,1},{1,0},{2,3},{3,2},{4,5},{5,4},{6,7},{7,6},{8,9},{9,8},{10,11... | collective-permute-start | bytes 49160 | tf_op jit(solution)/shard_map/ppermute | solution.py:364
  18.8 0.0 collective-permute-start.5
  18.8 2.0 %collective-permute-done.4.corner_first_ref = f32[4,1024]{1,0:T(4,128)S(1)} collective-permute-done((f32[4,1024]{1,0:T(4,128)S(1)}, f32[4,1024]{1,0:T(4,128)S(1)}, u32[]{:S(2)}, u32[]{:S(2)}) %collective-permute-start.4) | collective-permute-done | bytes 16416 | tf_op jit(solution)/shard_map/ppermute | solution.py:364
  20.8 0.0 collective-permute-done.5.corner_second_ref
  20.8 2.6 %all-to-all-done.sketch_ref = f32[16,4,128]{2,1,0:T(4,128)S(1)} async-done(((f32[16,4,128]{2,1,0:T(4,128)}), f32[16,4,128]{2,1,0:T(4,128)S(1)}, u32[]{:S(2)}, u32[]{:S(2)}) %all-to-all-start) | async-done | bytes 32800 | tf_op jit(solution)/shard_map/all_to_all | solution.py:370
  23.4 1.2 %shard_map.71 = (f32[4,8,1024]{2,1,0:T(8,128)}, f32[4,8,1024]{2,1,0:T(8,128)}) custom-call(f32[16,4,128]{2,1,0:T(4,128)S(1)} %all-to-all-done.sketch_ref, f32[4,8,1024]{2,1,0:T(8,128)S(1)} %get-tuple-element.21.b_ref, f32[4,8,1024]{2,1,0:T(8,128)S(1)} %get-tuple-element.35.image_ref, f32[4,8,1024]{2,1,0:T(8,128)S(1)} %get-tuple-element.36.twice_ref, ...), custom_call_target="tpu_custom_call" | custom-call | tf_op jit(solution)/shard_map/pallas_call | solution.py:341
Async XLA Ops:
  2.1 6.3 %collective-permute-start = (f32[28,1024]{1,0:T(8,128)S(1)}, f32[28,1024]{1,0:T(8,128)S(1)}, u32[]{:S(2)}, u32[]{:S(2)}) collective-permute-start(f32[28,1024]{1,0:T(8,128)S(1)} %get-tuple-element.27), channel_id=1, source_target_pairs={{0,1},{1,0},{2,3},{3,2},{4,8},{5,9},{6,10},{7,11},{8,4},{9,5},{10,... | collective-permute-start | bytes 344072 | tf_op jit(solution)/shard_map/ppermute | solution.py:364
  5.2 3.2 %collective-permute-start.1 = (f32[28,1024]{1,0:T(8,128)S(1)}, f32[28,1024]{1,0:T(8,128)S(1)}, u32[]{:S(2)}, u32[]{:S(2)}) collective-permute-start(f32[28,1024]{1,0:T(8,128)S(1)} %get-tuple-element.28), channel_id=1, source_target_pairs={{0,4},{1,5},{2,6},{3,7},{4,0},{5,1},{6,2},{7,3},{8,12},{9,13},{10,... | collective-permute-start | bytes 344072 | tf_op jit(solution)/shard_map/ppermute | solution.py:364
  5.2 4.0 %collective-permute-start.2 = (f32[16,1024]{1,0:T(8,128)S(1)}, f32[16,1024]{1,0:T(8,128)S(1)}, u32[]{:S(2)}, u32[]{:S(2)}) collective-permute-start(f32[16,1024]{1,0:T(8,128)S(1)} %get-tuple-element.31), channel_id=1, source_target_pairs={{0,4},{1,2},{2,1},{3,7},{4,0},{5,6},{6,5},{7,3},{8,12},{9,10},{10,... | collective-permute-start | bytes 196616 | tf_op jit(solution)/shard_map/ppermute | solution.py:364
  5.7 5.1 %collective-permute-start.3 = (f32[16,1024]{1,0:T(8,128)S(1)}, f32[16,1024]{1,0:T(8,128)S(1)}, u32[]{:S(2)}, u32[]{:S(2)}) collective-permute-start(f32[16,1024]{1,0:T(8,128)S(1)} %get-tuple-element.32), channel_id=1, source_target_pairs={{0,1},{1,0},{2,3},{3,2},{4,5},{5,4},{6,7},{7,6},{8,9},{9,8},{10,11... | collective-permute-start | bytes 196616 | tf_op jit(solution)/shard_map/ppermute | solution.py:364
  12.7 10.6 %all-to-all-start = ((f32[16,4,128]{2,1,0:T(4,128)}), f32[16,4,128]{2,1,0:T(4,128)S(1)}, u32[]{:S(2)}, u32[]{:S(2)}) async-start(f32[16,4,128]{2,1,0:T(4,128)} %broadcast_in_dim.2), calls=%async_computation | async-start | bytes 65536 | tf_op jit(solution)/shard_map/all_to_all | solution.py:370
  16.9 3.9 %collective-permute-start.4 = (f32[4,1024]{1,0:T(4,128)S(1)}, f32[4,1024]{1,0:T(4,128)S(1)}, u32[]{:S(2)}, u32[]{:S(2)}) collective-permute-start(f32[4,1024]{1,0:T(4,128)S(1)} %get-tuple-element.38), channel_id=1, source_target_pairs={{0,1},{1,0},{2,3},{3,2},{4,5},{5,4},{6,7},{7,6},{8,9},{9,8},{10,11... | collective-permute-start | bytes 49160 | tf_op jit(solution)/shard_map/ppermute | solution.py:364
  18.8 2.0 %collective-permute-start.5 = (f32[4,1024]{1,0:T(4,128)S(1)}, f32[4,1024]{1,0:T(4,128)S(1)}, u32[]{:S(2)}, u32[]{:S(2)}) collective-permute-start(f32[4,1024]{1,0:T(4,128)S(1)} %get-tuple-element.39), channel_id=1, source_target_pairs={{0,4},{1,2},{2,1},{3,7},{4,0},{5,6},{6,5},{7,3},{8,12},{9,10},{10,... | collective-permute-start | bytes 49160 | tf_op jit(solution)/shard_map/ppermute | solution.py:364
where the time goes:
time: 24.8 us; the launch traced here: 24.6 us
  starting transfers between devices  12.4 us (50%)
  waiting for transfers between devices  6.18 us (25%)
  Pallas kernels  4.76 us (19%)
  between operations  0.66 us (3%)
  local copies, waits for them, and re-layouts  0.64 us (3%)
    ppermute x6, starting transfers between devices, swap(): return lax.ppermute(array, ('gx', 'gy'), pairs)  8.23 us
    pallas_call x4, Pallas kernels, call(): pl.pallas_call(kernel, out_shape=[jax.ShapeDtypeStruct(shape, jnp.float32...  4.76 us
    all_to_all x1, starting transfers between devices, everyones(): return lax.all_to_all(copies, ('gx', 'gy'), 0, 0)  4.13 us
    ppermute x6, waiting for transfers between devices, swap(): return lax.ppermute(array, ('gx', 'gy'), pairs)  3.61 us
    all_to_all x1, waiting for transfers between devices, everyones(): return lax.all_to_all(copies, ('gx', 'gy'), 0, 0)  2.56 us
    broadcast_in_dim x1, local copies, waits for them, and re-layouts, everyones(): copies = jnp.broadcast_to(sketch[None], (count,) + sketch.shape)  0.64 us
  transfers between devices with their start and end apart: 7, of which 3 were waited for; matrix products, arithmetic and copies ran while one was open for 0% of the time, Pallas kernels for 3%

commit v1 on v0

--- a/solution.py
+++ b/solution.py
@@ -291,7 +291,7 @@
     sketch_ref, b_ref, image_ref, twice_ref, ends_ref, corner_first_ref, corner_second_ref,
     solution_ref, residual_ref,
 ):
-    sketches = jnp.sum(sketch_ref[...], axis=0)
+    sketches = sketch_ref[...]
 
     def inner(first, second):
         return jnp.sum(first * second, axis=1, keepdims=True)
@@ -364,10 +364,13 @@
     return lax.ppermute(array, ("gx", "gy"), pairs)
 
 
-def everyones(sketch):
-    count = lax.axis_size("gx") * lax.axis_size("gy")
-    copies = jnp.broadcast_to(sketch[None], (count,) + sketch.shape)
-    return lax.all_to_all(copies, ("gx", "gy"), 0, 0)
+def sum_over(table, axis):
+    count = lax.axis_size(axis)
+    others = [
+        lax.ppermute(table, axis, [(i, i ^ step) for i in range(count)])
+        for step in range(1, count)
+    ]
+    return sum(others, table)
 
 
 def body(b, warmth, phase, slots, draw):
@@ -409,7 +412,7 @@
         flops=work,
     )
     got_corners = [swap(array, "gy", turn) for turn, array in enumerate((first, second))]
-    sketches = everyones(sketch)
+    sketches = sum_over(sum_over(sketch, "gx"), "gy")
     return tuple(
         call(last_kernel, [block, block], sketches, b, image, twice, ends, *got_corners)
     )

time: 24.8 us -> 25.4 us (1.024)
  starting transfers between devices: 12.4 us -> 13.6 us
  local copies, waits for them, and re-layouts: 0.64 us -> 0 us
    ppermute x0 -> x6, starting transfers between devices: none -> 6.32 us  [sum_over(): lax.ppermute(table, axis, [(i, i ^ step) for i in range(count)])]
    all_to_all x1 -> x0, starting transfers between devices: 4.13 us -> none  [everyones(): return lax.all_to_all(copies, ('gx', 'gy'), 0, 0)]
    ppermute x0 -> x6, waiting for transfers between devices: none -> 3.72 us  [sum_over(): lax.ppermute(table, axis, [(i, i ^ step) for i in range(count)])]
    all_to_all x1 -> x0, waiting for transfers between devices: 2.56 us -> none  [everyones(): return lax.all_to_all(copies, ('gx', 'gy'), 0, 0)]
    ppermute x6, waiting for transfers between devices: 3.61 us -> 2.47 us  [swap(): return lax.ppermute(array, ('gx', 'gy'), pairs)]
    ppermute x6, starting transfers between devices: 8.23 us -> 7.24 us  [swap(): return lax.ppermute(array, ('gx', 'gy'), pairs)]
    broadcast_in_dim x1 -> x0, local copies, waits for them, and re-layouts: 0.64 us -> none  [everyones(): copies = jnp.broadcast_to(sketch[None], (count,) + sketch.shape)]
  transfers between devices with their start and end apart: 7 -> 12, of which waited for: 3 -> 6; matrix products, arithmetic and copies ran while one was open for 0% -> 0% of each run, Pallas kernels for 3% -> 3%
where the time goes in v1:
time: 25.4 us; the launch traced here: 25.2 us
  starting transfers between devices  13.6 us (54%)
  waiting for transfers between devices  6.19 us (24%)
  Pallas kernels  4.78 us (19%)
  between operations  0.66 us (3%)
    ppermute x6, starting transfers between devices, swap(): return lax.ppermute(array, ('gx', 'gy'), pairs)  7.24 us
    ppermute x6, starting transfers between devices, sum_over(): lax.ppermute(table, axis, [(i, i ^ step) for i in range(count)])  6.32 us
    pallas_call x4, Pallas kernels, call(): pl.pallas_call(kernel, out_shape=[jax.ShapeDtypeStruct(shape, jnp.float32...  4.78 us
    ppermute x6, waiting for transfers between devices, sum_over(): lax.ppermute(table, axis, [(i, i ^ step) for i in range(count)])  3.72 us
    ppermute x6, waiting for transfers between devices, swap(): return lax.ppermute(array, ('gx', 'gy'), pairs)  2.47 us
  transfers between devices with their start and end apart: 12, of which 6 were waited for; matrix products, arithmetic and copies ran while one was open for 0% of the time, Pallas kernels for 3%

profile of v1, /device:TPU:0, one launch (start us, length us, event | category | flops | bytes accessed | tf_op | source)
XLA Modules:
  0.0 25.2 jit_solution(2040178872435382222)
XLA Ops:
  0.6 1.5 %shard_map.68 = (f32[4,8,1024]{2,1,0:T(8,128)S(1)}, f32[4,8,1024]{2,1,0:T(8,128)S(1)}, f32[4,8,1024]{2,1,0:T(8,128)S(1)}, f32[4,8,1024]{2,1,0:T(8,128)S(1)}, f32...) custom-call(f32[4,8,1024]{2,1,0:T(8,128)} %b_hbm.1, ...), custom_call_target="tpu_custom_call" | custom-call | tf_op jit(solution)/shard_map/pallas_call | solution.py:341
  2.1 3.1 %collective-permute-start = (f32[28,1024]{1,0:T(8,128)S(1)}, f32[28,1024]{1,0:T(8,128)S(1)}, u32[]{:S(2)}, u32[]{:S(2)}) collective-permute-start(f32[28,1024]{1,0:T(8,128)S(1)} %get-tuple-element.27), channel_id=1, source_target_pairs={{0,1},{1,0},{2,3},{3,2},{4,8},{5,9},{6,10},{7,11},{8,4},{9,5},{10,... | collective-permute-start | bytes 344072 | tf_op jit(solution)/shard_map/ppermute | solution.py:364
  5.2 0.1 collective-permute-start.1
  5.2 0.5 %collective-permute-start.2 = (f32[16,1024]{1,0:T(8,128)S(1)}, f32[16,1024]{1,0:T(8,128)S(1)}, u32[]{:S(2)}, u32[]{:S(2)}) collective-permute-start(f32[16,1024]{1,0:T(8,128)S(1)} %get-tuple-element.31), channel_id=1, source_target_pairs={{0,4},{1,2},{2,1},{3,7},{4,0},{5,6},{6,5},{7,3},{8,12},{9,10},{10,... | collective-permute-start | bytes 196616 | tf_op jit(solution)/shard_map/ppermute | solution.py:364
  5.7 2.7 %collective-permute-start.3 = (f32[16,1024]{1,0:T(8,128)S(1)}, f32[16,1024]{1,0:T(8,128)S(1)}, u32[]{:S(2)}, u32[]{:S(2)}) collective-permute-start(f32[16,1024]{1,0:T(8,128)S(1)} %get-tuple-element.32), channel_id=1, source_target_pairs={{0,1},{1,0},{2,3},{3,2},{4,5},{5,4},{6,7},{7,6},{8,9},{9,8},{10,11... | collective-permute-start | bytes 196616 | tf_op jit(solution)/shard_map/ppermute | solution.py:364
  8.4 0.0 collective-permute-done.got_second_ref.x_second_ref
  8.4 0.0 collective-permute-done.1.got_first_ref.x_first_ref
  8.4 0.8 %shard_map.69 = (f32[6,8,1024]{2,1,0:T(8,128)S(1)}, f32[4,8,1024]{2,1,0:T(8,128)S(1)}, f32[8,128]{1,0:T(8,128)S(1)}) custom-call(f32[4,8,1024]{2,1,0:T(8,128)S(1)} %get-tuple-element.21.b_ref, f32[4,8,1024]{2,1,0:T(8,128)S(1)} %get-tuple-element.22.cond_ref, f32[4,8,1024]{2,1,0:T(8,128)S(1)} %get-tuple-element.23.cap_ref, ...), custom_call_target="tpu_custom_call" | custom-call | flops 25165824 | tf_op jit(solution)/shard_map/pallas_call | solution.py:341
  9.2 1.6 %collective-permute-done.3.y_first_ref = f32[16,1024]{1,0:T(8,128)S(1)} collective-permute-done((f32[16,1024]{1,0:T(8,128)S(1)}, f32[16,1024]{1,0:T(8,128)S(1)}, u32[]{:S(2)}, u32[]{:S(2)}) %collective-permute-start.3) | collective-permute-done | bytes 65568 | tf_op jit(solution)/shard_map/ppermute | solution.py:364
  10.8 1.2 %shard_map.70 = (f32[4,8,1024]{2,1,0:T(8,128)S(1)}, f32[4,8,1024]{2,1,0:T(8,128)S(1)}, f32[4,128]{1,0:T(4,128)S(1)}, f32[4,1024]{1,0:T(4,128)S(1)}, f32[4,1024]{1,0:T(4,128)S(1)}, /*index=5*/f32[24,1024]{1,0:T(8,128)S(1)}) custom-call(f32[4,8,1024]{2,1,0:T(8,128)S(1)} %get-tuple-element.21.b_ref, f32[4,8,1024]{2,1,0:T(8,128)S(1)} %get-tuple-element.22.cond_ref, ...), custom_call_target="tpu_custom_call" | custom-call | flops 25165824 | tf_op jit(solution)/shard_map/pallas_call | solution.py:341
  12.1 0.0 collective-permute-start.6
  12.1 1.3 %collective-permute-start.5 = (f32[4,128]{1,0:T(4,128)S(1)}, f32[4,128]{1,0:T(4,128)S(1)}, u32[]{:S(2)}, u32[]{:S(2)}) collective-permute-start(f32[4,128]{1,0:T(4,128)S(1)} %get-tuple-element.34), channel_id=1, source_target_pairs={{0,8},{4,12},{8,0},{12,4},{1,9},{5,13},{9,1},{13,5},{2,10},{6,14},... | collective-permute-start | bytes 6152 | tf_op jit(solution)/shard_map/ppermute | solution.py:370
  13.4 0.6 %collective-permute-start.4 = (f32[4,128]{1,0:T(4,128)S(1)}, f32[4,128]{1,0:T(4,128)S(1)}, u32[]{:S(2)}, u32[]{:S(2)}) collective-permute-start(f32[4,128]{1,0:T(4,128)S(1)} %get-tuple-element.34), channel_id=1, source_target_pairs={{0,4},{4,0},{8,12},{12,8},{1,5},{5,1},{9,13},{13,9},{2,6},{6,2},{1... | collective-permute-start | bytes 6152 | tf_op jit(solution)/shard_map/ppermute | solution.py:370
  14.0 1.1 %collective-permute-done.6 = f32[4,128]{1,0:T(4,128)S(1)} collective-permute-done((f32[4,128]{1,0:T(4,128)S(1)}, f32[4,128]{1,0:T(4,128)S(1)}, u32[]{:S(2)}, u32[]{:S(2)}) %collective-permute-start.6) | collective-permute-done | bytes 2080 | tf_op jit(solution)/shard_map/ppermute | solution.py:370
  15.1 0.7 %collective-permute-done.5 = f32[4,128]{1,0:T(4,128)S(1)} collective-permute-done((f32[4,128]{1,0:T(4,128)S(1)}, f32[4,128]{1,0:T(4,128)S(1)}, u32[]{:S(2)}, u32[]{:S(2)}) %collective-permute-start.5) | collective-permute-done | bytes 2080 | tf_op jit(solution)/shard_map/ppermute | solution.py:370
  15.8 0.0 collective-permute-done.4
  15.8 2.8 %collective-permute-start.9 = (f32[4,128]{1,0:T(4,128)S(1)}, f32[4,128]{1,0:T(4,128)S(1)}, u32[]{:S(2)}, u32[]{:S(2)}) collective-permute-start(f32[4,128]{1,0:T(4,128)S(1)} %add_add_fusion.1), channel_id=1, source_target_pairs={{0,3},{1,2},{2,1},{3,0},{4,7},{5,6},{6,5},{7,4},{8,11},{9,10},{10,... | collective-permute-start | bytes 6152 | tf_op jit(solution)/shard_map/ppermute | solution.py:370
  18.6 0.5 %collective-permute-start.8 = (f32[4,128]{1,0:T(4,128)S(1)}, f32[4,128]{1,0:T(4,128)S(1)}, u32[]{:S(2)}, u32[]{:S(2)}) collective-permute-start(f32[4,128]{1,0:T(4,128)S(1)} %add_add_fusion.1), channel_id=1, source_target_pairs={{0,2},{1,3},{2,0},{3,1},{4,6},{5,7},{6,4},{7,5},{8,10},{9,11},{10,... | collective-permute-start | bytes 6152 | tf_op jit(solution)/shard_map/ppermute | solution.py:370
  19.1 1.1 %collective-permute-start.7 = (f32[4,128]{1,0:T(4,128)S(1)}, f32[4,128]{1,0:T(4,128)S(1)}, u32[]{:S(2)}, u32[]{:S(2)}) collective-permute-start(f32[4,128]{1,0:T(4,128)S(1)} %add_add_fusion.1), channel_id=1, source_target_pairs={{0,1},{1,0},{2,3},{3,2},{4,5},{5,4},{6,7},{7,6},{8,9},{9,8},{10,11... | collective-permute-start | bytes 6152 | tf_op jit(solution)/shard_map/ppermute | solution.py:370
  20.2 0.9 %collective-permute-start.10 = (f32[4,1024]{1,0:T(4,128)S(1)}, f32[4,1024]{1,0:T(4,128)S(1)}, u32[]{:S(2)}, u32[]{:S(2)}) collective-permute-start(f32[4,1024]{1,0:T(4,128)S(1)} %get-tuple-element.38), channel_id=1, source_target_pairs={{0,1},{1,0},{2,3},{3,2},{4,5},{5,4},{6,7},{7,6},{8,9},{9,8},{10,11... | collective-permute-start | bytes 49160 | tf_op jit(solution)/shard_map/ppermute | solution.py:364
  21.2 0.1 collective-permute-done.9
  21.2 1.9 %collective-permute-done.8 = f32[4,128]{1,0:T(4,128)S(1)} collective-permute-done((f32[4,128]{1,0:T(4,128)S(1)}, f32[4,128]{1,0:T(4,128)S(1)}, u32[]{:S(2)}, u32[]{:S(2)}) %collective-permute-start.8) | collective-permute-done | bytes 2080 | tf_op jit(solution)/shard_map/ppermute | solution.py:370
  23.1 0.9 %collective-permute-done.10.corner_first_ref = f32[4,1024]{1,0:T(4,128)S(1)} collective-permute-done((f32[4,1024]{1,0:T(4,128)S(1)}, f32[4,1024]{1,0:T(4,128)S(1)}, u32[]{:S(2)}, u32[]{:S(2)}) %collective-permute-start.10) | collective-permute-done | bytes 16416 | tf_op jit(solution)/shard_map/ppermute | solution.py:364
  24.0 1.2 %shard_map.71 = (f32[4,8,1024]{2,1,0:T(8,128)}, f32[4,8,1024]{2,1,0:T(8,128)}) custom-call(f32[4,128]{1,0:T(4,128)S(1)} %add_add_fusion.sketch_ref, f32[4,8,1024]{2,1,0:T(8,128)S(1)} %get-tuple-element.21.b_ref, f32[4,8,1024]{2,1,0:T(8,128)S(1)} %get-tuple-element.35.image_ref, f32[4,8,1024]{2,1,0:T(8,128)S(1)} %get-tuple-element.36.twice_ref, ...), custom_call_target="tpu_custom_call" | custom-call | tf_op jit(solution)/shard_map/pallas_call | solution.py:341
  (6 shorter events, 0.0 us)
Async XLA Ops:
  2.1 6.3 %collective-permute-start = (f32[28,1024]{1,0:T(8,128)S(1)}, f32[28,1024]{1,0:T(8,128)S(1)}, u32[]{:S(2)}, u32[]{:S(2)}) collective-permute-start(f32[28,1024]{1,0:T(8,128)S(1)} %get-tuple-element.27), channel_id=1, source_target_pairs={{0,1},{1,0},{2,3},{3,2},{4,8},{5,9},{6,10},{7,11},{8,4},{9,5},{10,... | collective-permute-start | bytes 344072 | tf_op jit(solution)/shard_map/ppermute | solution.py:364
  5.2 3.2 %collective-permute-start.1 = (f32[28,1024]{1,0:T(8,128)S(1)}, f32[28,1024]{1,0:T(8,128)S(1)}, u32[]{:S(2)}, u32[]{:S(2)}) collective-permute-start(f32[28,1024]{1,0:T(8,128)S(1)} %get-tuple-element.28), channel_id=1, source_target_pairs={{0,4},{1,5},{2,6},{3,7},{4,0},{5,1},{6,2},{7,3},{8,12},{9,13},{10,... | collective-permute-start | bytes 344072 | tf_op jit(solution)/shard_map/ppermute | solution.py:364
  5.2 4.0 %collective-permute-start.2 = (f32[16,1024]{1,0:T(8,128)S(1)}, f32[16,1024]{1,0:T(8,128)S(1)}, u32[]{:S(2)}, u32[]{:S(2)}) collective-permute-start(f32[16,1024]{1,0:T(8,128)S(1)} %get-tuple-element.31), channel_id=1, source_target_pairs={{0,4},{1,2},{2,1},{3,7},{4,0},{5,6},{6,5},{7,3},{8,12},{9,10},{10,... | collective-permute-start | bytes 196616 | tf_op jit(solution)/shard_map/ppermute | solution.py:364
  5.7 5.1 %collective-permute-start.3 = (f32[16,1024]{1,0:T(8,128)S(1)}, f32[16,1024]{1,0:T(8,128)S(1)}, u32[]{:S(2)}, u32[]{:S(2)}) collective-permute-start(f32[16,1024]{1,0:T(8,128)S(1)} %get-tuple-element.32), channel_id=1, source_target_pairs={{0,1},{1,0},{2,3},{3,2},{4,5},{5,4},{6,7},{7,6},{8,9},{9,8},{10,11... | collective-permute-start | bytes 196616 | tf_op jit(solution)/shard_map/ppermute | solution.py:364
  12.1 3.0 %collective-permute-start.6 = (f32[4,128]{1,0:T(4,128)S(1)}, f32[4,128]{1,0:T(4,128)S(1)}, u32[]{:S(2)}, u32[]{:S(2)}) collective-permute-start(f32[4,128]{1,0:T(4,128)S(1)} %get-tuple-element.34), channel_id=1, source_target_pairs={{0,12},{4,8},{8,4},{12,0},{1,13},{5,9},{9,5},{13,1},{2,14},{6,10},... | collective-permute-start | bytes 6152 | tf_op jit(solution)/shard_map/ppermute | solution.py:370
  12.1 3.7 %collective-permute-start.5 = (f32[4,128]{1,0:T(4,128)S(1)}, f32[4,128]{1,0:T(4,128)S(1)}, u32[]{:S(2)}, u32[]{:S(2)}) collective-permute-start(f32[4,128]{1,0:T(4,128)S(1)} %get-tuple-element.34), channel_id=1, source_target_pairs={{0,8},{4,12},{8,0},{12,4},{1,9},{5,13},{9,1},{13,5},{2,10},{6,14},... | collective-permute-start | bytes 6152 | tf_op jit(solution)/shard_map/ppermute | solution.py:370
  13.4 2.4 %collective-permute-start.4 = (f32[4,128]{1,0:T(4,128)S(1)}, f32[4,128]{1,0:T(4,128)S(1)}, u32[]{:S(2)}, u32[]{:S(2)}) collective-permute-start(f32[4,128]{1,0:T(4,128)S(1)} %get-tuple-element.34), channel_id=1, source_target_pairs={{0,4},{4,0},{8,12},{12,8},{1,5},{5,1},{9,13},{13,9},{2,6},{6,2},{1... | collective-permute-start | bytes 6152 | tf_op jit(solution)/shard_map/ppermute | solution.py:370
  15.8 5.4 %collective-permute-start.9 = (f32[4,128]{1,0:T(4,128)S(1)}, f32[4,128]{1,0:T(4,128)S(1)}, u32[]{:S(2)}, u32[]{:S(2)}) collective-permute-start(f32[4,128]{1,0:T(4,128)S(1)} %add_add_fusion.1), channel_id=1, source_target_pairs={{0,3},{1,2},{2,1},{3,0},{4,7},{5,6},{6,5},{7,4},{8,11},{9,10},{10,... | collective-permute-start | bytes 6152 | tf_op jit(solution)/shard_map/ppermute | solution.py:370
  18.6 4.5 %collective-permute-start.8 = (f32[4,128]{1,0:T(4,128)S(1)}, f32[4,128]{1,0:T(4,128)S(1)}, u32[]{:S(2)}, u32[]{:S(2)}) collective-permute-start(f32[4,128]{1,0:T(4,128)S(1)} %add_add_fusion.1), channel_id=1, source_target_pairs={{0,2},{1,3},{2,0},{3,1},{4,6},{5,7},{6,4},{7,5},{8,10},{9,11},{10,... | collective-permute-start | bytes 6152 | tf_op jit(solution)/shard_map/ppermute | solution.py:370
  19.1 3.9 %collective-permute-start.7 = (f32[4,128]{1,0:T(4,128)S(1)}, f32[4,128]{1,0:T(4,128)S(1)}, u32[]{:S(2)}, u32[]{:S(2)}) collective-permute-start(f32[4,128]{1,0:T(4,128)S(1)} %add_add_fusion.1), channel_id=1, source_target_pairs={{0,1},{1,0},{2,3},{3,2},{4,5},{5,4},{6,7},{7,6},{8,9},{9,8},{10,11... | collective-permute-start | bytes 6152 | tf_op jit(solution)/shard_map/ppermute | solution.py:370
  20.2 3.7 %collective-permute-start.10 = (f32[4,1024]{1,0:T(4,128)S(1)}, f32[4,1024]{1,0:T(4,128)S(1)}, u32[]{:S(2)}, u32[]{:S(2)}) collective-permute-start(f32[4,1024]{1,0:T(4,128)S(1)} %get-tuple-element.38), channel_id=1, source_target_pairs={{0,1},{1,0},{2,3},{3,2},{4,5},{5,4},{6,7},{7,6},{8,9},{9,8},{10,11... | collective-permute-start | bytes 49160 | tf_op jit(solution)/shard_map/ppermute | solution.py:364
  21.2 2.8 %collective-permute-start.11 = (f32[4,1024]{1,0:T(4,128)S(1)}, f32[4,1024]{1,0:T(4,128)S(1)}, u32[]{:S(2)}, u32[]{:S(2)}) collective-permute-start(f32[4,1024]{1,0:T(4,128)S(1)} %get-tuple-element.39), channel_id=1, source_target_pairs={{0,4},{1,2},{2,1},{3,7},{4,0},{5,6},{6,5},{7,3},{8,12},{9,10},{10,... | collective-permute-start | bytes 49160 | tf_op jit(solution)/shard_map/ppermute | solution.py:364

commit v2 on v1

--- a/solution.py
+++ b/solution.py
@@ -221,7 +221,7 @@
 def third_kernel(
     b_ref, cond_ref, cap_ref, draw_ref, slot_ref, wide_ref, beside_ref, x_second_ref,
     x_first_ref, y_second_ref, y_first_ref, inside_ref, image_ref, twice_ref, sketch_ref,
-    corner_first_ref, corner_second_ref, ends_ref, cells_ref, extra_ref,
+    first_ref, second_ref, ends_ref, cells_ref, extra_ref,
 ):
     planes, rows, depth = b_ref.shape
     index = lax.broadcasted_iota(jnp.int32, (rows, depth), 0)
@@ -279,16 +279,15 @@
     extra, nothing = [extra_ref[k] for k in range(3)], jnp.zeros((8, depth), jnp.float32)
     cells.append(((nothing, nothing, extra[0]), extra[1], extra[2], range(8)))
     sketch = inside_ref[...] + sketch_rows(cells, cells_ref)
-    sketch_ref[...] = sketch[: FIELDS + 1]
+    for ref in (sketch_ref, first_ref, second_ref):
+        ref[:, :SKETCH] = sketch[: FIELDS + 1]
     for k, plane in enumerate((b_wide[0], b_wide[-1], c_wide[0], c_wide[-1])):
-        at = slice(k, k + 1)
-        corner_first_ref[at], corner_second_ref[at] = by_turn(
-            plane[:1], plane[rows - 1 :], "gy"
-        )
+        at = slice(k, k + 1), slice(SKETCH, None)
+        first_ref[at], second_ref[at] = by_turn(plane[:1], plane[rows - 1 :], "gy")
 
 
 def last_kernel(
-    sketch_ref, b_ref, image_ref, twice_ref, ends_ref, corner_first_ref, corner_second_ref,
+    sketch_ref, b_ref, image_ref, twice_ref, ends_ref, got_first_ref, got_second_ref,
     solution_ref, residual_ref,
 ):
     sketches = sketch_ref[...]
@@ -323,7 +322,7 @@
         b, image = b_ref[i], image_ref[i]
         solution_ref[i] = c0 * b + c1 * image
         residual_ref[i] = b - c0 * image - c1 * twice_ref[i]
-    corners = by_turn(corner_first_ref[...], corner_second_ref[...], "gy")
+    corners = by_turn(got_first_ref[:, SKETCH:], got_second_ref[:, SKETCH:], "gy")
     for side, (j, here, corner) in enumerate(zip((0, rows - 1), has_beside("gy"), corners)):
         for end, i in enumerate((0, planes - 1)):
             b, cond = corner[end : end + 1], corner[2 + end : 3 + end]
@@ -364,13 +363,19 @@
     return lax.ppermute(array, ("gx", "gy"), pairs)
 
 
-def sum_over(table, axis):
+def meet(array, axis, turn):
     count = lax.axis_size(axis)
-    others = [
-        lax.ppermute(table, axis, [(i, i ^ step) for i in range(count)])
-        for step in range(1, count)
-    ]
-    return sum(others, table)
+
+    def partner(player, turn):
+        if player in (turn, count - 1):
+            return count - 1 if player == turn else turn
+        return (2 * turn - player) % (count - 1)
+
+    players = [count - 1]
+    while len(players) < count:
+        players.append(partner(players[-1], (len(players) - 1) % 2))
+    pairs = [(i, players.index(partner(player, turn))) for i, player in enumerate(players)]
+    return lax.ppermute(array, axis, pairs)
 
 
 def body(b, warmth, phase, slots, draw):
@@ -404,17 +409,21 @@
         scratch=[cells],
         flops=work,
     )
+    message = (FIELDS + 1, SKETCH + depth)
     image, twice, sketch, first, second, ends = call(
         third_kernel,
-        [block, block, (FIELDS + 1, SKETCH), corner, corner, (24, depth)],
+        [block, block, (FIELDS + 1, SKETCH), message, message, (24, depth)],
         b, cond, cap, draw, slots, image_wide, beside, *got_x, *got_y, inside,
         scratch=[cells, pltpu.VMEM((3, 8, depth), jnp.float32)],
         flops=work,
     )
-    got_corners = [swap(array, "gy", turn) for turn, array in enumerate((first, second))]
-    sketches = sum_over(sum_over(sketch, "gx"), "gy")
+    first, second = meet(first, "gy", 0), meet(second, "gy", 1)
+    others = [meet(sketch, "gy", turn) for turn in range(2, lax.axis_size("gy") - 1)]
+    sketch = sum(others, sketch + first[:, :SKETCH] + second[:, :SKETCH])
+    others = [meet(sketch, "gx", turn) for turn in range(lax.axis_size("gx") - 1)]
+    sketch = sum(others, sketch)
     return tuple(
-        call(last_kernel, [block, block], sketches, b, image, twice, ends, *got_corners)
+        call(last_kernel, [block, block], sketch, b, image, twice, ends, first, second)
     )
 
 

time: 25.4 us -> 25 us (0.984)
  starting transfers between devices: 13.6 us -> 12 us
  waiting for transfers between devices: 6.19 us -> 7.44 us
    ppermute x6, waiting for transfers between devices: 3.72 us -> 5.84 us  [meet(): return lax.ppermute(array, axis, pairs)]
    ppermute x6 -> x4, starting transfers between devices: 7.24 us -> 6.3 us  [swap(): return lax.ppermute(array, ('gx', 'gy'), pairs)]
    ppermute x6 -> x4, waiting for transfers between devices: 2.47 us -> 1.61 us  [swap(): return lax.ppermute(array, ('gx', 'gy'), pairs)]
    ppermute x6, starting transfers between devices: 6.32 us -> 5.72 us  [meet(): return lax.ppermute(array, axis, pairs)]
  transfers between devices with their start and end apart: 12 -> 10, of which waited for: 6 -> 4; matrix products, arithmetic and copies ran while one was open for 0% -> 0% of each run, Pallas kernels for 3% -> 3%
where the time goes in v2:
time: 25 us; the launch traced here: 24.9 us
  starting transfers between devices  12 us (48%)
  waiting for transfers between devices  7.44 us (30%)
  Pallas kernels  4.74 us (19%)
  between operations  0.66 us (3%)
    ppermute x4, starting transfers between devices, swap(): return lax.ppermute(array, ('gx', 'gy'), pairs)  6.3 us
    ppermute x6, waiting for transfers between devices, meet(): return lax.ppermute(array, axis, pairs)  5.84 us
    ppermute x6, starting transfers between devices, meet(): return lax.ppermute(array, axis, pairs)  5.72 us
    pallas_call x4, Pallas kernels, call(): pl.pallas_call(kernel, out_shape=[jax.ShapeDtypeStruct(shape, jnp.float32...  4.74 us
    ppermute x4, waiting for transfers between devices, swap(): return lax.ppermute(array, ('gx', 'gy'), pairs)  1.61 us
  transfers between devices with their start and end apart: 10, of which 4 were waited for; matrix products, arithmetic and copies ran while one was open for 0% of the time, Pallas kernels for 3%

profile of v2, /device:TPU:0, one launch (start us, length us, event | category | flops | bytes accessed | tf_op | source)
XLA Modules:
  0.0 24.9 jit_solution(4113966095047749675)
XLA Ops:
  0.6 1.5 %shard_map.68 = (f32[4,8,1024]{2,1,0:T(8,128)S(1)}, f32[4,8,1024]{2,1,0:T(8,128)S(1)}, f32[4,8,1024]{2,1,0:T(8,128)S(1)}, f32[4,8,1024]{2,1,0:T(8,128)S(1)}, f32...) custom-call(f32[4,8,1024]{2,1,0:T(8,128)} %b_hbm.1, ...), custom_call_target="tpu_custom_call" | custom-call | tf_op jit(solution)/shard_map/pallas_call | solution.py:340
  2.1 3.1 %collective-permute-start = (f32[28,1024]{1,0:T(8,128)S(1)}, f32[28,1024]{1,0:T(8,128)S(1)}, u32[]{:S(2)}, u32[]{:S(2)}) collective-permute-start(f32[28,1024]{1,0:T(8,128)S(1)} %get-tuple-element.27), channel_id=1, source_target_pairs={{0,1},{1,0},{2,3},{3,2},{4,8},{5,9},{6,10},{7,11},{8,4},{9,5},{10,... | collective-permute-start | bytes 344072 | tf_op jit(solution)/shard_map/ppermute | solution.py:363
  5.2 0.1 collective-permute-start.1
  5.2 0.5 %collective-permute-start.2 = (f32[16,1024]{1,0:T(8,128)S(1)}, f32[16,1024]{1,0:T(8,128)S(1)}, u32[]{:S(2)}, u32[]{:S(2)}) collective-permute-start(f32[16,1024]{1,0:T(8,128)S(1)} %get-tuple-element.31), channel_id=1, source_target_pairs={{0,4},{1,2},{2,1},{3,7},{4,0},{5,6},{6,5},{7,3},{8,12},{9,10},{10,... | collective-permute-start | bytes 196616 | tf_op jit(solution)/shard_map/ppermute | solution.py:363
  5.7 2.7 %collective-permute-start.3 = (f32[16,1024]{1,0:T(8,128)S(1)}, f32[16,1024]{1,0:T(8,128)S(1)}, u32[]{:S(2)}, u32[]{:S(2)}) collective-permute-start(f32[16,1024]{1,0:T(8,128)S(1)} %get-tuple-element.32), channel_id=1, source_target_pairs={{0,1},{1,0},{2,3},{3,2},{4,5},{5,4},{6,7},{7,6},{8,9},{9,8},{10,11... | collective-permute-start | bytes 196616 | tf_op jit(solution)/shard_map/ppermute | solution.py:363
  8.4 0.0 collective-permute-done.got_second_ref.x_second_ref
  8.4 0.0 collective-permute-done.1.got_first_ref.x_first_ref
  8.4 0.8 %shard_map.69 = (f32[6,8,1024]{2,1,0:T(8,128)S(1)}, f32[4,8,1024]{2,1,0:T(8,128)S(1)}, f32[8,128]{1,0:T(8,128)S(1)}) custom-call(f32[4,8,1024]{2,1,0:T(8,128)S(1)} %get-tuple-element.21.b_ref, f32[4,8,1024]{2,1,0:T(8,128)S(1)} %get-tuple-element.22.cond_ref, f32[4,8,1024]{2,1,0:T(8,128)S(1)} %get-tuple-element.23.cap_ref, ...), custom_call_target="tpu_custom_call" | custom-call | flops 25165824 | tf_op jit(solution)/shard_map/pallas_call | solution.py:340
  9.2 0.0 collective-permute-done.2.y_second_ref
  9.2 1.6 %collective-permute-done.3.y_first_ref = f32[16,1024]{1,0:T(8,128)S(1)} collective-permute-done((f32[16,1024]{1,0:T(8,128)S(1)}, f32[16,1024]{1,0:T(8,128)S(1)}, u32[]{:S(2)}, u32[]{:S(2)}) %collective-permute-start.3) | collective-permute-done | bytes 65568 | tf_op jit(solution)/shard_map/ppermute | solution.py:363
  10.8 1.2 %shard_map.70 = (f32[4,8,1024]{2,1,0:T(8,128)S(1)}, f32[4,8,1024]{2,1,0:T(8,128)S(1)}, f32[4,128]{1,0:T(4,128)S(1)}, f32[4,1152]{1,0:T(4,128)S(1)}, f32[4,1152]{1,0:T(4,128)S(1)}, /*index=5*/f32[24,1024]{1,0:T(8,128)S(1)}) custom-call(f32[4,8,1024]{2,1,0:T(8,128)S(1)} %get-tuple-element.21.b_ref, f32[4,8,1024]{2,1,0:T(8,128)S(1)} %get-tuple-element.22.cond_ref, ...), custom_call_target="tpu_custom_call" | custom-call | flops 25165824 | tf_op jit(solution)/shard_map/pallas_call | solution.py:340
  12.0 1.9 %collective-permute-start.4 = (f32[4,1152]{1,0:T(4,128)S(1)}, f32[4,1152]{1,0:T(4,128)S(1)}, u32[]{:S(2)}, u32[]{:S(2)}) collective-permute-start(f32[4,1152]{1,0:T(4,128)S(1)} %get-tuple-element.35), channel_id=1, source_target_pairs={{0,1},{1,0},{2,3},{3,2},{4,5},{5,4},{6,7},{7,6},{8,9},{9,8},{10,11... | collective-permute-start | bytes 55304 | tf_op jit(solution)/shard_map/ppermute | solution.py:378
  13.9 1.4 %collective-permute-start.5 = (f32[4,1152]{1,0:T(4,128)S(1)}, f32[4,1152]{1,0:T(4,128)S(1)}, u32[]{:S(2)}, u32[]{:S(2)}) collective-permute-start(f32[4,1152]{1,0:T(4,128)S(1)} %get-tuple-element.36), channel_id=1, source_target_pairs={{0,3},{1,2},{2,1},{3,0},{4,7},{5,6},{6,5},{7,4},{8,11},{9,10},{10,... | collective-permute-start | bytes 55304 | tf_op jit(solution)/shard_map/ppermute | solution.py:378
  15.3 0.3 %collective-permute-start.6 = (f32[4,128]{1,0:T(4,128)S(1)}, f32[4,128]{1,0:T(4,128)S(1)}, u32[]{:S(2)}, u32[]{:S(2)}) collective-permute-start(f32[4,128]{1,0:T(4,128)S(1)} %get-tuple-element.34), channel_id=1, source_target_pairs={{0,2},{1,3},{2,0},{3,1},{4,6},{5,7},{6,4},{7,5},{8,10},{9,11},{10,... | collective-permute-start | bytes 6152 | tf_op jit(solution)/shard_map/ppermute | solution.py:378
  15.6 4.2 %collective-permute-done.6 = f32[4,128]{1,0:T(4,128)S(1)} collective-permute-done((f32[4,128]{1,0:T(4,128)S(1)}, f32[4,128]{1,0:T(4,128)S(1)}, u32[]{:S(2)}, u32[]{:S(2)}) %collective-permute-start.6) | collective-permute-done | bytes 2080 | tf_op jit(solution)/shard_map/ppermute | solution.py:378
  19.8 0.0 collective-permute-done.4.got_first_ref
  19.8 0.0 collective-permute-done.5.got_second_ref
  19.8 0.8 %collective-permute-start.9 = (f32[4,128]{1,0:T(4,128)S(1)}, f32[4,128]{1,0:T(4,128)S(1)}, u32[]{:S(2)}, u32[]{:S(2)}) collective-permute-start(f32[4,128]{1,0:T(4,128)S(1)} %fusion), channel_id=1, source_target_pairs={{0,8},{4,12},{8,0},{12,4},{1,9},{5,13},{9,1},{13,5},{2,10},{6,14},... | collective-permute-start | bytes 6152 | tf_op jit(solution)/shard_map/ppermute | solution.py:378
  20.6 0.0 collective-permute-start.8
  20.6 1.4 %collective-permute-start.7 = (f32[4,128]{1,0:T(4,128)S(1)}, f32[4,128]{1,0:T(4,128)S(1)}, u32[]{:S(2)}, u32[]{:S(2)}) collective-permute-start(f32[4,128]{1,0:T(4,128)S(1)} %fusion), channel_id=1, source_target_pairs={{0,4},{4,0},{8,12},{12,8},{1,5},{5,1},{9,13},{13,9},{2,6},{6,2},{1... | collective-permute-start | bytes 6152 | tf_op jit(solution)/shard_map/ppermute | solution.py:378
  22.0 1.4 %collective-permute-done.9 = f32[4,128]{1,0:T(4,128)S(1)} collective-permute-done((f32[4,128]{1,0:T(4,128)S(1)}, f32[4,128]{1,0:T(4,128)S(1)}, u32[]{:S(2)}, u32[]{:S(2)}) %collective-permute-start.9) | collective-permute-done | bytes 2080 | tf_op jit(solution)/shard_map/ppermute | solution.py:378
  23.4 0.2 collective-permute-done.8
  23.6 0.0 collective-permute-done.7
  23.6 1.2 %shard_map.71 = (f32[4,8,1024]{2,1,0:T(8,128)}, f32[4,8,1024]{2,1,0:T(8,128)}) custom-call(f32[4,128]{1,0:T(4,128)S(1)} %add_add_fusion.sketch_ref, f32[4,8,1024]{2,1,0:T(8,128)S(1)} %get-tuple-element.21.b_ref, f32[4,8,1024]{2,1,0:T(8,128)S(1)} %get-tuple-element.37.image_ref, f32[4,8,1024]{2,1,0:T(8,128)S(1)} %get-tuple-element.38.twice_ref, ...), custom_call_target="tpu_custom_call" | custom-call | tf_op jit(solution)/shard_map/pallas_call | solution.py:340
  (2 shorter events, 0.0 us)
Async XLA Ops:
  2.1 6.3 %collective-permute-start = (f32[28,1024]{1,0:T(8,128)S(1)}, f32[28,1024]{1,0:T(8,128)S(1)}, u32[]{:S(2)}, u32[]{:S(2)}) collective-permute-start(f32[28,1024]{1,0:T(8,128)S(1)} %get-tuple-element.27), channel_id=1, source_target_pairs={{0,1},{1,0},{2,3},{3,2},{4,8},{5,9},{6,10},{7,11},{8,4},{9,5},{10,... | collective-permute-start | bytes 344072 | tf_op jit(solution)/shard_map/ppermute | solution.py:363
  5.2 3.2 %collective-permute-start.1 = (f32[28,1024]{1,0:T(8,128)S(1)}, f32[28,1024]{1,0:T(8,128)S(1)}, u32[]{:S(2)}, u32[]{:S(2)}) collective-permute-start(f32[28,1024]{1,0:T(8,128)S(1)} %get-tuple-element.28), channel_id=1, source_target_pairs={{0,4},{1,5},{2,6},{3,7},{4,0},{5,1},{6,2},{7,3},{8,12},{9,13},{10,... | collective-permute-start | bytes 344072 | tf_op jit(solution)/shard_map/ppermute | solution.py:363
  5.2 4.0 %collective-permute-start.2 = (f32[16,1024]{1,0:T(8,128)S(1)}, f32[16,1024]{1,0:T(8,128)S(1)}, u32[]{:S(2)}, u32[]{:S(2)}) collective-permute-start(f32[16,1024]{1,0:T(8,128)S(1)} %get-tuple-element.31), channel_id=1, source_target_pairs={{0,4},{1,2},{2,1},{3,7},{4,0},{5,6},{6,5},{7,3},{8,12},{9,10},{10,... | collective-permute-start | bytes 196616 | tf_op jit(solution)/shard_map/ppermute | solution.py:363
  5.7 5.1 %collective-permute-start.3 = (f32[16,1024]{1,0:T(8,128)S(1)}, f32[16,1024]{1,0:T(8,128)S(1)}, u32[]{:S(2)}, u32[]{:S(2)}) collective-permute-start(f32[16,1024]{1,0:T(8,128)S(1)} %get-tuple-element.32), channel_id=1, source_target_pairs={{0,1},{1,0},{2,3},{3,2},{4,5},{5,4},{6,7},{7,6},{8,9},{9,8},{10,11... | collective-permute-start | bytes 196616 | tf_op jit(solution)/shard_map/ppermute | solution.py:363
  12.0 7.7 %collective-permute-start.4 = (f32[4,1152]{1,0:T(4,128)S(1)}, f32[4,1152]{1,0:T(4,128)S(1)}, u32[]{:S(2)}, u32[]{:S(2)}) collective-permute-start(f32[4,1152]{1,0:T(4,128)S(1)} %get-tuple-element.35), channel_id=1, source_target_pairs={{0,1},{1,0},{2,3},{3,2},{4,5},{5,4},{6,7},{7,6},{8,9},{9,8},{10,11... | collective-permute-start | bytes 55304 | tf_op jit(solution)/shard_map/ppermute | solution.py:378
  13.9 5.9 %collective-permute-start.5 = (f32[4,1152]{1,0:T(4,128)S(1)}, f32[4,1152]{1,0:T(4,128)S(1)}, u32[]{:S(2)}, u32[]{:S(2)}) collective-permute-start(f32[4,1152]{1,0:T(4,128)S(1)} %get-tuple-element.36), channel_id=1, source_target_pairs={{0,3},{1,2},{2,1},{3,0},{4,7},{5,6},{6,5},{7,4},{8,11},{9,10},{10,... | collective-permute-start | bytes 55304 | tf_op jit(solution)/shard_map/ppermute | solution.py:378
  15.3 4.5 %collective-permute-start.6 = (f32[4,128]{1,0:T(4,128)S(1)}, f32[4,128]{1,0:T(4,128)S(1)}, u32[]{:S(2)}, u32[]{:S(2)}) collective-permute-start(f32[4,128]{1,0:T(4,128)S(1)} %get-tuple-element.34), channel_id=1, source_target_pairs={{0,2},{1,3},{2,0},{3,1},{4,6},{5,7},{6,4},{7,5},{8,10},{9,11},{10,... | collective-permute-start | bytes 6152 | tf_op jit(solution)/shard_map/ppermute | solution.py:378
  19.8 3.7 %collective-permute-start.9 = (f32[4,128]{1,0:T(4,128)S(1)}, f32[4,128]{1,0:T(4,128)S(1)}, u32[]{:S(2)}, u32[]{:S(2)}) collective-permute-start(f32[4,128]{1,0:T(4,128)S(1)} %fusion), channel_id=1, source_target_pairs={{0,8},{4,12},{8,0},{12,4},{1,9},{5,13},{9,1},{13,5},{2,10},{6,14},... | collective-permute-start | bytes 6152 | tf_op jit(solution)/shard_map/ppermute | solution.py:378
  20.6 3.0 %collective-permute-start.8 = (f32[4,128]{1,0:T(4,128)S(1)}, f32[4,128]{1,0:T(4,128)S(1)}, u32[]{:S(2)}, u32[]{:S(2)}) collective-permute-start(f32[4,128]{1,0:T(4,128)S(1)} %fusion), channel_id=1, source_target_pairs={{0,12},{4,8},{8,4},{12,0},{1,13},{5,9},{9,5},{13,1},{2,14},{6,10},... | collective-permute-start | bytes 6152 | tf_op jit(solution)/shard_map/ppermute | solution.py:378
  20.6 3.0 %collective-permute-start.7 = (f32[4,128]{1,0:T(4,128)S(1)}, f32[4,128]{1,0:T(4,128)S(1)}, u32[]{:S(2)}, u32[]{:S(2)}) collective-permute-start(f32[4,128]{1,0:T(4,128)S(1)} %fusion), channel_id=1, source_target_pairs={{0,4},{4,0},{8,12},{12,8},{1,5},{5,1},{9,13},{13,9},{2,6},{6,2},{1... | collective-permute-start | bytes 6152 | tf_op jit(solution)/shard_map/ppermute | solution.py:378
